TPU v7x, 32 devices: a whole 2x2x4 slice. The times are simulated.
32 devices in a mesh: groups: 2 (over x), seq: 16 (over z, y, core).
Axes of the slice: x: 2, y: 2, z: 4, core: 2. Of those that a mesh axis runs over, the one named last changes fastest.
Arguments:
- patches: bfloat16 [4096, 1176], P(('groups', 'seq')), parts along dimension 0, may hold values from -6 to 6
- row_owner: int32 [4096, 1], P(('groups', 'seq')), parts along dimension 0, may hold values from 0 to 15; in each aligned block of 128 rows (0 to 127, 128 to 255, ...) at most 16 rows name the same one
- window_slot: int32 [4096], P(('groups', 'seq')), parts along dimension 0, may hold values from 0 to 3
- w_patch: bfloat16 [1176, 1280], replicated, may hold values from -1 to 1
- vit_gain: float32 [1280], replicated, may hold values from 0.1 to 1.9
- w_qkv: bfloat16 [1280, 1920], replicated, may hold values from -1 to 1
- queries: bfloat16 [4096, 4096], P(('groups', 'seq')), parts along dimension 0, may hold values from -36 to 36
- new_kv: bfloat16 [4096, 1024], P(('groups', 'seq')), parts along dimension 0, may hold values from -6 to 6
- kv_cache: bfloat16 [2048, 16, 1024], P(('groups', 'seq')), parts along dimension 0, may hold values from -6 to 6
- block_table: int32 [32, 64], P(('groups', 'seq')), parts along dimension 0, may hold values from -1 to 1023, as said below
Outputs:
- vision_out: bfloat16 [4096, 640], P(('groups', 'seq')), parts along dimension 0
- attention_out: bfloat16 [4096, 4096], P(('groups', 'seq')), parts along dimension 0
There are 2 independent parts, one for each index of `groups`. A program takes and returns all parts, laid end to end along the dimension named above; an argument that names none is the same for every part. Nothing has to cross between parts.
Inputs may be any that keep to these rules, and one draw needn't show every extreme that they name: `row_owner`: in the rows of one device, each owner is named by at most 16 rows. `block_table`: block b is stored on device b // 64. Each row lists 8 or more distinct blocks, then -1 entries; at most 8 of a row's blocks lie on one device.
All inputs are finite; a program needn't handle non-finite values.
Results may differ from a plain program's by a relative error of at most 0.0093.
Values may be sent and summed in bfloat16 or wider, within the bound.
No kernel may reach another device: no remote copies, remote signals or barrier semaphores. Data moves between devices by JAX's collectives and lax.ppermute only.
A program may use at most 64 MiB of HBM per device.

v0:
```python
import jax
import jax.numpy as jnp
from jax import lax
from jax.sharding import PartitionSpec as P

VHEADS = 8
VHD = 80
QHEADS = 32
KVH = 4
HD = 128


def embed_rows(patch_rows, w_patch, vit_gain):
    embedded = jnp.dot(patch_rows, w_patch, preferred_element_type=jnp.float32).astype(jnp.bfloat16)
    widened = lax.optimization_barrier(embedded).astype(jnp.float32)
    factor = lax.rsqrt(jnp.mean(widened * widened, axis=1, keepdims=True) + 1e-06)
    return (widened * factor * vit_gain).astype(jnp.bfloat16)


def window_attention(qkv_rows, windows):
    total_rows = qkv_rows.shape[0]
    inner_width = VHEADS * VHD
    query_heads = qkv_rows[:, :inner_width].reshape(total_rows, VHEADS, VHD)
    key_heads = qkv_rows[:, inner_width : 2 * inner_width].reshape(total_rows, VHEADS, VHD)
    value_heads = qkv_rows[:, 2 * inner_width :].reshape(total_rows, VHEADS, VHD)
    is_live = windows >= 0
    block_rows = min(512, total_rows)
    every_row = jnp.arange(total_rows)
    scores = jnp.einsum(
        "qhd,khd->hqk", query_heads, key_heads, preferred_element_type=jnp.float32
    ) * VHD ** (-0.5)
    row_ids = 0 + jnp.arange(block_rows)
    allowed = (windows[0:block_rows, None] == windows[None, :]) & is_live[None, :] | (
        row_ids[:, None] == every_row[None, :]
    )
    scores = jnp.where(allowed[None], scores, -jnp.inf)
    highest = jnp.max(scores, axis=2, keepdims=True)
    weights = jnp.exp(scores - highest)
    totals = jnp.sum(weights, axis=2)
    blended = jnp.einsum(
        "hqk,khd->qhd",
        weights.astype(jnp.bfloat16),
        value_heads,
        preferred_element_type=jnp.float32,
    )
    pieces = (blended / totals.T[:, :, None]).reshape(block_rows, inner_width)
    return pieces.astype(jnp.bfloat16)


def prompt_attention(query_rows, fresh_kv, cached_kv, cached_live):
    token_count = query_rows.shape[0]
    kv_width = KVH * HD
    group_size = QHEADS // KVH
    every_kv = jnp.concatenate([cached_kv, fresh_kv], axis=0)
    causal = jnp.arange(token_count)[None, :] <= jnp.arange(token_count)[:, None]
    allowed = jnp.concatenate(
        [jnp.broadcast_to(cached_live[None, :], (token_count, cached_live.shape[0])), causal],
        axis=1,
    )
    outputs = []
    for head_group in range(KVH):
        query_heads = query_rows[
            :, head_group * group_size * HD : (head_group + 1) * group_size * HD
        ]
        query_heads = query_heads.reshape(token_count, group_size, HD)
        key_head = every_kv[:, head_group * HD : (head_group + 1) * HD]
        value_head = every_kv[:, kv_width + head_group * HD : kv_width + (head_group + 1) * HD]
        scores = jnp.einsum(
            "cpd,kd->cpk", query_heads, key_head, preferred_element_type=jnp.float32
        ) * HD ** (-0.5)
        scores = jnp.where(allowed[:, None, :], scores, -jnp.inf)
        highest = jnp.max(scores, axis=2, keepdims=True)
        weights = jnp.exp(scores - highest)
        totals = jnp.sum(weights, axis=2)
        blended = jnp.einsum(
            "cpk,kd->cpd",
            weights.astype(jnp.bfloat16),
            value_head,
            preferred_element_type=jnp.float32,
        )
        outputs.append((blended / totals[:, :, None]).reshape(token_count, group_size * HD))
    return jnp.concatenate(outputs, axis=1).astype(jnp.bfloat16)


def shards(
    patches,
    row_owner,
    window_slot,
    w_patch,
    vit_gain,
    w_qkv,
    queries,
    new_kv,
    kv_cache,
    block_table,
):
    devices = lax.axis_size("seq")
    src_rows = patches.shape[0]
    capacity = 2 * src_rows // devices
    slot_count = devices * capacity
    owner_ids = row_owner[:, 0]
    owner_hits = (owner_ids[:, None] == jnp.arange(devices)[None, :]).astype(jnp.bfloat16)
    strictly_lower = (jnp.arange(src_rows)[:, None] > jnp.arange(src_rows)[None, :]).astype(
        jnp.bfloat16
    )
    earlier = jnp.dot(strictly_lower, owner_hits, preferred_element_type=jnp.float32)
    ranks = jnp.sum(earlier * owner_hits.astype(jnp.float32), axis=1).astype(jnp.int32)
    target_slot = owner_ids * capacity + ranks
    window_buffer = (
        jnp.full((slot_count,), -1, jnp.int32)
        .at[target_slot]
        .set(window_slot)
        .reshape(devices, capacity)
    )
    normed = embed_rows(patches, w_patch, vit_gain)
    outgoing = jnp.zeros((slot_count, normed.shape[1]), jnp.bfloat16).at[target_slot].set(normed)
    arrived, arrived_windows = (
        lax.all_to_all(
            outgoing.reshape(devices, capacity, -1), "seq", split_axis=0, concat_axis=0, tiled=True
        ),
        lax.all_to_all(window_buffer, "seq", split_axis=0, concat_axis=0, tiled=True),
    )
    qkv_rows = jnp.dot(
        arrived.reshape(slot_count, -1), w_qkv, preferred_element_type=jnp.float32
    ).astype(jnp.bfloat16)
    attended = window_attention(qkv_rows, arrived_windows.reshape(slot_count))
    returned = lax.all_to_all(
        attended.reshape(devices, capacity, -1), "seq", split_axis=0, concat_axis=0, tiled=True
    )
    vision_out = returned.reshape(slot_count, -1)[target_slot]
    table_row = block_table[0]
    table_len = table_row.shape[0]
    blocks_dev = kv_cache.shape[0]
    block_tokens = kv_cache.shape[1]
    per_owner = 2 * table_len // devices
    is_live = table_row >= 0
    holder = jnp.where(is_live, table_row // blocks_dev, -1)
    local_block = jnp.where(is_live, table_row % blocks_dev, 0)
    before_entry = jnp.arange(table_len)[:, None] > jnp.arange(table_len)[None, :]
    same_holder = (holder[:, None] == holder[None, :]) & is_live[None, :] & before_entry
    holder_rank = jnp.sum(same_holder.astype(jnp.int32), axis=1)
    request_slot = jnp.where(is_live, holder * per_owner + holder_rank, devices * per_owner)
    wanted = (
        jnp.full((devices * per_owner,), -1, jnp.int32)
        .at[request_slot]
        .set(local_block, mode="drop")
        .reshape(devices, per_owner)
    )
    asked = lax.all_to_all(wanted, "seq", split_axis=0, concat_axis=0, tiled=True)
    fetched = kv_cache[jnp.maximum(asked, 0)]
    delivered = lax.all_to_all(fetched, "seq", split_axis=0, concat_axis=0, tiled=True)
    cached_kv = delivered.reshape(devices * per_owner * block_tokens, -1)
    cached_live = jnp.repeat(wanted.reshape(-1) >= 0, block_tokens)
    attention_out = prompt_attention(queries, new_kv, cached_kv, cached_live)
    return (vision_out, attention_out)


def solution(mesh):
    in_specs = (
        P(("groups", "seq"), None),
        P(("groups", "seq"), None),
        P(("groups", "seq")),
        P(),
        P(),
        P(),
        P(("groups", "seq"), None),
        P(("groups", "seq"), None),
        P(("groups", "seq"), None, None),
        P(("groups", "seq"), None),
    )
    out_specs = (P(("groups", "seq"), None), P(("groups", "seq"), None))
    return jax.shard_map(shards, mesh=mesh, in_specs=in_specs, out_specs=out_specs, check_vma=False)
```

profile of v0, /device:TPU:13, one launch (start us, length us, event | category | flops | bytes accessed | tf_op | source)
XLA Modules:
  0.0 194.3 jit_solution(9243506905654627205)
XLA Ops:
  4.1 6.6 %all-to-all-start.1 = ((s32[16,1,16]{2,1,0:T(1,128)}), s32[16,1,16]{2,1,0:T(1,128)S(1)}, u32[]{:S(2)}, u32[]{:S(2)}) async-start(s32[16,1,16]{2,1,0:T(1,128)} %all_to_all.22), calls=%async_computation.1 | async-start | bytes 16384 | tf_op jit(solution)/shard_map/all_to_all | solution.py:121
  11.3 1.6 convolution_convert_fusion.1
  13.1 2.3 %scatter_custom_fusion = bf16[256,1280]{1,0:T(8,128)(2,1)} fusion(s32[128]{0:T(128)S(1)} %fusion.94, bf16[128,1280]{1,0:T(8,128)(2,1)S(1)} %convolution_convert_fusion.1, f32[1280]{0:T(1024)} %param.14, f32[128]{0:T(128)S(1)} %add_rsqrt_fusion, bf16[]{:T(256)} %constant.18.clone.1), kind=kCustom, calls=%fused_computation.91 | custom fusion | flops 655360 | bytes 988674 | tf_op jit(solution)/shard_map/scatter | solution.py:116
  15.4 6.0 %all-to-all-start = ((bf16[16,16,1280]{2,1,0:T(8,128)(2,1)}), bf16[16,16,1280]{2,1,0:T(8,128)(2,1)S(1)}, u32[]{:S(2)}, u32[]{:S(2)}) async-start(bf16[16,16,1280]{2,1,0:T(8,128)(2,1)} %bitcast.3), calls=%async_computation | async-start | bytes 1310720 | tf_op jit(solution)/shard_map/all_to_all | solution.py:118
  24.7 13.2 %all-to-all-done = bf16[16,16,1280]{2,1,0:T(8,128)(2,1)S(1)} async-done(((bf16[16,16,1280]{2,1,0:T(8,128)(2,1)}), bf16[16,16,1280]{2,1,0:T(8,128)(2,1)S(1)}, u32[]{:S(2)}, u32[]{:S(2)}) %all-to-all-start) | async-done | bytes 655392 | tf_op jit(solution)/shard_map/all_to_all | solution.py:118
  37.8 5.0 %all-to-all-start.3 = ((s32[16,1,8]{2,1,0:T(1,128)}), s32[16,1,8]{2,1,0:T(1,128)S(1)}, u32[]{:S(2)}, u32[]{:S(2)}) async-start(s32[16,1,8]{2,1,0:T(1,128)} %bitcast.17), calls=%async_computation.3 | async-start | bytes 16384 | tf_op jit(solution)/shard_map/all_to_all | solution.py:149
  42.8 3.9 %convolution_convert_fusion = bf16[256,1920]{1,0:T(8,128)(2,1)S(1)} fusion(bf16[256,1280]{1,0:T(8,128)(2,1)S(1)} %bitcast.130, bf16[1280,1920]{1,0:T(8,128)(2,1)} %param.15), kind=kOutput, calls=%fused_computation.36 | convolution fusion | flops 1258782720 | bytes 6553600 | tf_op jit(solution)/shard_map/dot_general | solution.py:123
  50.4 6.0 %all-to-all-start.2 = ((bf16[16,16,640]{2,1,0:T(8,128)(2,1)}), bf16[16,16,640]{2,1,0:T(8,128)(2,1)S(1)}, u32[]{:S(2)}, u32[]{:S(2)}) async-start(bf16[16,16,640]{2,1,0:T(8,128)(2,1)} %convert_element_type.68), calls=%async_computation.2 | async-start | bytes 655360 | tf_op jit(solution)/shard_map/all_to_all | solution.py:127
  56.6 2.8 %gather_fusion.1 = bf16[128,16,1024]{2,1,0:T(8,128)(2,1)} fusion(bf16[64,16,1024]{2,1,0:T(8,128)(2,1)S(1)} %copy-done.3, s32[1024]{0:T(1024)S(1)} %pad_clamp_fusion), kind=kCustom, calls=%fused_computation.1 | custom fusion | bytes 8389120 | tf_op jit(solution)/shard_map/gather | solution.py:150
  59.4 6.4 %all-to-all-done.2 = bf16[16,16,640]{2,1,0:T(8,128)(2,1)S(1)} async-done(((bf16[16,16,640]{2,1,0:T(8,128)(2,1)}), bf16[16,16,640]{2,1,0:T(8,128)(2,1)S(1)}, u32[]{:S(2)}, u32[]{:S(2)}) %all-to-all-start.2) | async-done | bytes 327712 | tf_op jit(solution)/shard_map/all_to_all | solution.py:127
  65.8 6.1 %all-to-all-start.4 = ((bf16[16,8,16,1024]{3,2,1,0:T(8,128)(2,1)}), bf16[16,8,16,1024]{3,2,1,0:T(8,128)(2,1)}, u32[]{:S(2)}, u32[]{:S(2)}) async-start(bf16[16,8,16,1024]{3,2,1,0:T(8,128)(2,1)} %bitcast.118), calls=%async_computation.4 | async-start | bytes 8388608 | tf_op jit(solution)/shard_map/all_to_all | solution.py:151
  73.1 2.2 %pad_add_fusion = pred[128,2176]{0,1:T(8,128)(4,1)S(1)} fusion(pred[128,128]{0,1:T(8,128)(4,1)S(1)} %iota_compare_fusion.1, pred[2176]{0:T(1024)(128)(4,1)S(1)} %pad.6.clone), kind=kLoop, calls=%fused_computation.61 | loop fusion | flops 278528 | bytes 297088 | tf_op jit(solution)/shard_map/concatenate | solution.py:56
  75.3 1.5 gather_fusion
  76.8 87.6 %all-to-all-done.4 = bf16[16,8,16,1024]{3,2,1,0:T(8,128)(2,1)} async-done(((bf16[16,8,16,1024]{3,2,1,0:T(8,128)(2,1)}), bf16[16,8,16,1024]{3,2,1,0:T(8,128)(2,1)}, u32[]{:S(2)}, u32[]{:S(2)}) %all-to-all-start.4) | async-done | bytes 4194336 | tf_op jit(solution)/shard_map/all_to_all | solution.py:151
  164.4 2.4 %fusion.115 = (f32[128,8]{0,1:T(8,128)S(1)}, f32[128,8,2176]{0,2,1:T(8,128)S(1)}) fusion(bf16[128,8,128]{0,2,1:T(8,128)(2,1)S(1)} %bitcast.123, bf16[128,1024]{1,0:T(8,128)(2,1)S(1)} %copy-done.2, bf16[2048,1024]{1,0:T(8,128)(2,1)} %bitcast.19, pred[128,2176]{0,1:T(8,128)(4,1)S(1)} %pad_add_fusion), kind=kOutput, calls=%fused_computation.159 | convolution fusion | flops 578223104 | bytes 13914112 | tf_op jit(solution)/shard_map/cpd,kd->cpk/dot_general | solution.py:68
  168.0 2.6 %fusion.28 = bf16[128,8,128]{0,2,1:T(8,128)(2,1)S(1)} fusion(f32[128,8,2176]{0,2,1:T(8,128)S(1)} %get-tuple-element.20, f32[128,8]{0,1:T(8,128)S(1)} %get-tuple-element.19, bf16[2048,1024]{1,0:T(8,128)(2,1)} %bitcast.19, bf16[128,1024]{1,0:T(8,128)(2,1)S(1)} %copy-done.2, f32[128,8]{0,1:T(8,128)S(1)} %fusion), kind=kOutput, calls=%fused_computation.54 | convolution fusion | flops 576258048 | bytes 13639680 | tf_op jit(solution)/shard_map/cpk,kd->cpd/dot_general | solution.py:75
  171.4 2.4 %fusion.114 = (f32[128,8]{0,1:T(8,128)S(1)}, f32[128,8,2176]{0,2,1:T(8,128)S(1)}) fusion(bf16[128,8,128]{0,2,1:T(8,128)(2,1)S(1)} %bitcast.122, bf16[128,1024]{1,0:T(8,128)(2,1)S(1)} %copy-done.2, bf16[2048,1024]{1,0:T(8,128)(2,1)} %bitcast.19, pred[128,2176]{0,1:T(8,128)(4,1)S(1)} %pad_add_fusion), kind=kOutput, calls=%fused_computation.158 | convolution fusion | flops 578223104 | bytes 13914112 | tf_op jit(solution)/shard_map/cpd,kd->cpk/dot_general | solution.py:68
  173.8 1.2 fusion.2
  175.0 2.6 %fusion.34 = bf16[128,8,128]{0,2,1:T(8,128)(2,1)S(1)} fusion(f32[128,8,2176]{0,2,1:T(8,128)S(1)} %get-tuple-element.18, f32[128,8]{0,1:T(8,128)S(1)} %get-tuple-element.17, bf16[2048,1024]{1,0:T(8,128)(2,1)} %bitcast.19, bf16[128,1024]{1,0:T(8,128)(2,1)S(1)} %copy-done.2, f32[128,8]{0,1:T(8,128)S(1)} %fusion.2), kind=kOutput, calls=%fused_computation.56 | convolution fusion | flops 576258048 | bytes 13639680 | tf_op jit(solution)/shard_map/cpk,kd->cpd/dot_general | solution.py:75
  178.4 2.4 %fusion.113 = (f32[128,8]{0,1:T(8,128)S(1)}, f32[128,8,2176]{0,2,1:T(8,128)S(1)}) fusion(bf16[128,8,128]{0,2,1:T(8,128)(2,1)S(1)} %bitcast.121, bf16[128,1024]{1,0:T(8,128)(2,1)S(1)} %copy-done.2, bf16[2048,1024]{1,0:T(8,128)(2,1)} %bitcast.19, pred[128,2176]{0,1:T(8,128)(4,1)S(1)} %pad_add_fusion), kind=kOutput, calls=%fused_computation.157 | convolution fusion | flops 578223104 | bytes 13914112 | tf_op jit(solution)/shard_map/cpd,kd->cpk/dot_general | solution.py:68
  182.0 2.8 %fusion.40 = bf16[128,8,128]{0,2,1:T(8,128)(2,1)S(1)} fusion(f32[128,8,2176]{0,2,1:T(8,128)S(1)} %get-tuple-element.16, f32[128,8]{0,1:T(8,128)S(1)} %get-tuple-element.15, bf16[2048,1024]{1,0:T(8,128)(2,1)} %bitcast.19, bf16[128,1024]{1,0:T(8,128)(2,1)S(1)} %copy-done.2, f32[128,8]{0,1:T(8,128)S(1)} %fusion.4), kind=kOutput, calls=%fused_computation.58 | convolution fusion | flops 576258048 | bytes 13639680 | tf_op jit(solution)/shard_map/cpk,kd->cpd/dot_general | solution.py:75
  185.6 2.4 %fusion.112 = (f32[128,8]{0,1:T(8,128)S(1)}, f32[128,8,2176]{0,2,1:T(8,128)S(1)}) fusion(bf16[128,8,128]{0,2,1:T(8,128)(2,1)S(1)} %bitcast.120, bf16[128,1024]{1,0:T(8,128)(2,1)S(1)} %copy-done.2, bf16[2048,1024]{1,0:T(8,128)(2,1)} %bitcast.19, pred[128,2176]{0,1:T(8,128)(4,1)S(1)} %pad_add_fusion), kind=kOutput, calls=%fused_computation.156 | convolution fusion | flops 578223104 | bytes 13914112 | tf_op jit(solution)/shard_map/cpd,kd->cpk/dot_general | solution.py:68
  189.2 2.8 %fusion.46 = bf16[128,8,128]{0,2,1:T(8,128)(2,1)S(1)} fusion(f32[128,8,2176]{0,2,1:T(8,128)S(1)} %get-tuple-element.14, f32[128,8]{0,1:T(8,128)S(1)} %get-tuple-element.13, bf16[128,1024]{1,0:T(8,128)(2,1)S(1)} %copy-done.2, bf16[2048,1024]{1,0:T(8,128)(2,1)} %bitcast.19, f32[128,8]{0,1:T(8,128)S(1)} %fusion.6), kind=kOutput, calls=%fused_computation.60 | convolution fusion | flops 576258048 | bytes 13639680 | tf_op jit(solution)/shard_map/cpk,kd->cpd/dot_general | solution.py:75
  192.1 2.2 %pad_maximum_fusion = bf16[128,4096]{1,0:T(8,128)(2,1)} fusion(bf16[128,1024]{1,0:T(8,128)(2,1)S(1)} %copy.105, bf16[128,1024]{1,0:T(8,128)(2,1)} %copy.104, bf16[128,1024]{1,0:T(8,128)(2,1)} %copy.103, bf16[128,1024]{1,0:T(8,128)(2,1)} %copy.102), kind=kLoop, calls=%fused_computation.64 | loop fusion | flops 4194304 | bytes 2097152 | tf_op jit(solution)/shard_map/concatenate | solution.py:82
  (62 shorter events, 18.5 us)
Async XLA Ops:
  0.6 10.7 %copy-start = (bf16[1176,1280]{1,0:T(8,128)(2,1)S(1)}, bf16[1176,1280]{1,0:T(8,128)(2,1)}, u32[]{:S(2)}) copy-start(bf16[1176,1280]{1,0:T(8,128)(2,1)} %param.13) | copy-start | bytes 9031684
  0.6 20.8 %copy-start.5 = (s32[1,64]{1,0:T(1,128)S(1)}, s32[1,64]{1,0:T(1,128)}, u32[]{:S(2)}) copy-start(s32[1,64]{1,0:T(1,128)} %param.19) | copy-start | bytes 772
  4.1 11.3 %all-to-all-start.1 = ((s32[16,1,16]{2,1,0:T(1,128)}), s32[16,1,16]{2,1,0:T(1,128)S(1)}, u32[]{:S(2)}, u32[]{:S(2)}) async-start(s32[16,1,16]{2,1,0:T(1,128)} %all_to_all.22), calls=%async_computation.1 | async-start | bytes 16384 | tf_op jit(solution)/shard_map/all_to_all | solution.py:121
  15.4 22.4 %all-to-all-start = ((bf16[16,16,1280]{2,1,0:T(8,128)(2,1)}), bf16[16,16,1280]{2,1,0:T(8,128)(2,1)S(1)}, u32[]{:S(2)}, u32[]{:S(2)}) async-start(bf16[16,16,1280]{2,1,0:T(8,128)(2,1)} %bitcast.3), calls=%async_computation | async-start | bytes 1310720 | tf_op jit(solution)/shard_map/all_to_all | solution.py:118
  37.8 12.6 %all-to-all-start.3 = ((s32[16,1,8]{2,1,0:T(1,128)}), s32[16,1,8]{2,1,0:T(1,128)S(1)}, u32[]{:S(2)}, u32[]{:S(2)}) async-start(s32[16,1,8]{2,1,0:T(1,128)} %bitcast.17), calls=%async_computation.3 | async-start | bytes 16384 | tf_op jit(solution)/shard_map/all_to_all | solution.py:149
  47.9 8.7 %copy-start.3 = (bf16[64,16,1024]{2,1,0:T(8,128)(2,1)S(1)}, bf16[64,16,1024]{2,1,0:T(8,128)(2,1)}, u32[]{:S(2)}) copy-start(bf16[64,16,1024]{2,1,0:T(8,128)(2,1)} %param.18) | copy-start | bytes 6291460
  50.4 15.4 %all-to-all-start.2 = ((bf16[16,16,640]{2,1,0:T(8,128)(2,1)}), bf16[16,16,640]{2,1,0:T(8,128)(2,1)S(1)}, u32[]{:S(2)}, u32[]{:S(2)}) async-start(bf16[16,16,640]{2,1,0:T(8,128)(2,1)} %convert_element_type.68), calls=%async_computation.2 | async-start | bytes 655360 | tf_op jit(solution)/shard_map/all_to_all | solution.py:127
  59.4 12.8 %copy-start.4 = (bf16[128,4096]{1,0:T(8,128)(2,1)S(1)}, bf16[128,4096]{1,0:T(8,128)(2,1)}, u32[]{:S(2)}) copy-start(bf16[128,4096]{1,0:T(8,128)(2,1)} %param.16) | copy-start | bytes 3145732
  65.8 98.6 %all-to-all-start.4 = ((bf16[16,8,16,1024]{3,2,1,0:T(8,128)(2,1)}), bf16[16,8,16,1024]{3,2,1,0:T(8,128)(2,1)}, u32[]{:S(2)}, u32[]{:S(2)}) async-start(bf16[16,8,16,1024]{3,2,1,0:T(8,128)(2,1)} %bitcast.118), calls=%async_computation.4 | async-start | bytes 8388608 | tf_op jit(solution)/shard_map/all_to_all | solution.py:151
  71.9 92.5 %copy-start.2 = (bf16[128,1024]{1,0:T(8,128)(2,1)S(1)}, bf16[128,1024]{1,0:T(8,128)(2,1)}, u32[]{:S(2)}) copy-start(bf16[128,1024]{1,0:T(8,128)(2,1)} %param.17) | copy-start | bytes 786436
  189.2 5.1 %copy-start.1 = (bf16[1176,1280]{1,0:T(8,128)(2,1)S(1)}, bf16[1176,1280]{1,0:T(8,128)(2,1)}, u32[]{:S(2)}) copy-start(bf16[1176,1280]{1,0:T(8,128)(2,1)} %param.13) | copy-start | bytes 9031684
where the time goes:
time: 195 us; the launch traced here: 194 us
  waiting for transfers between devices  107 us (55%)
  starting transfers between devices  29.7 us (15%)
  matrix products  27.9 us (14%)
  other arithmetic  14.4 us (7%)
  local copies, waits for them, and re-layouts  14.1 us (7%)
    all_to_all x1, waiting for transfers between devices, shards(): lax.all_to_all(fetched, 'seq', split_axis=0, concat_axis=0, tiled=True)  87.6 us
    all_to_all x1, waiting for transfers between devices, shards(): lax.all_to_all(outgoing.reshape(devices, capacity, -1), 'seq', split_axis...  13.2 us
    dot_general x4, matrix products, prompt_attention(): jnp.einsum('cpk,kd->cpd', weights.astype(jnp.bfloat16), value_head, prefe...  10.8 us
    dot_general x4, matrix products, prompt_attention(): jnp.einsum('cpd,kd->cpk', query_heads, key_head, preferred_element_type=j...  9.43 us
    all_to_all x1, starting transfers between devices, shards(): lax.all_to_all(window_buffer, 'seq', split_axis=0, concat_axis=0, tiled=T...  6.55 us
    all_to_all x1, waiting for transfers between devices, shards(): lax.all_to_all(attended.reshape(devices, capacity, -1), 'seq', split_axis...  6.43 us
    all_to_all x1, starting transfers between devices, shards(): lax.all_to_all(fetched, 'seq', split_axis=0, concat_axis=0, tiled=True)  6.13 us
    all_to_all x1, starting transfers between devices, shards(): lax.all_to_all(attended.reshape(devices, capacity, -1), 'seq', split_axis...  6.02 us
  transfers between devices with their start and end apart: 5, of which 3 were waited for; matrix products, arithmetic and copies ran while one was open for 12% of the time, Pallas kernels for 0%

commit v1 on v0

v1 whole, which is shorter than its diff:
```python
import functools

import jax
import jax.numpy as jnp
from jax import lax
from jax.experimental import pallas as pl
from jax.experimental.pallas import tpu as pltpu
from jax.sharding import PartitionSpec as P

VHEADS = 8
VHD = 80
QHEADS = 32
KVH = 4
HD = 128
LANES = 128
CHUNK_BLOCKS = 16
HEADS_TILE = 4
LOG2E = 1.4426950408889634
HIDDEN = -1e30
VMEM_BYTES = 48 * 1024 * 1024


def iota(shape, axis):
    return lax.broadcasted_iota(jnp.int32, shape, axis)


def count(hits, axis):
    return jnp.sum(hits.astype(jnp.float32), axis=axis, keepdims=True).astype(jnp.int32)


def as_row(column):
    size = column.shape[0]
    diagonal = iota((size, size), 0) == iota((size, size), 1)
    return jnp.sum(jnp.where(diagonal, column, 0).astype(jnp.float32), axis=0, keepdims=True).astype(jnp.int32)


def as_column(row):
    size = row.shape[1]
    diagonal = iota((size, size), 0) == iota((size, size), 1)
    return jnp.sum(jnp.where(diagonal, row, 0).astype(jnp.float32), axis=1, keepdims=True).astype(jnp.int32)


def embed_kernel(
    capacity,
    per_owner,
    blocks_dev,
    patches_ref,
    w_ref,
    gain_ref,
    owner_ref,
    window_ref,
    table_ref,
    payload_ref,
    target_ref,
    request_ref,
    live_ref,
    embedded_ref,
):
    step = pl.program_id(0)
    width = w_ref.shape[1]
    piece = jnp.dot(patches_ref[...], w_ref[...], preferred_element_type=jnp.float32)
    embedded_ref[:, pl.ds(pl.multiple_of(step * width, width), width)] = piece.astype(jnp.bfloat16)

    @pl.when(step == pl.num_programs(0) - 1)
    def _():
        slots = payload_ref.shape[0]
        vit = embedded_ref.shape[1]
        rows = owner_ref.shape[0]
        owner_column = owner_ref[...]
        owner_row = as_row(owner_column)
        same = owner_column == owner_row
        first, second = iota((rows, rows), 0), iota((rows, rows), 1)
        rank_row = count(same & (first < second), 0)
        rank_column = count(same & (second < first), 1)
        target_ref[...] = owner_column * capacity + rank_column
        placed = (owner_row * capacity + rank_row) == iota((slots, rows), 0)
        windows = jnp.sum(
            jnp.where(placed, window_ref[...] + 1, 0).astype(jnp.float32), axis=1, keepdims=True
        )

        table_row = table_ref[...]
        entries = table_row.shape[1]
        live_row = table_row >= 0
        holder_row = jnp.where(live_row, table_row // blocks_dev, -1)
        local_row = jnp.where(live_row, table_row % blocks_dev, 0)
        holder_column = as_column(holder_row)
        before = iota((entries, entries), 0) < iota((entries, entries), 1)
        holder_rank = count((holder_column == holder_row) & before, 0)
        request_row = jnp.where(live_row, holder_row * per_owner + holder_rank, -1)
        first_request = jnp.sum(
            jnp.where(iota((1, entries), 1) == 0, request_row, 0).astype(jnp.float32),
            axis=1,
            keepdims=True,
        ).astype(jnp.int32)
        request_ref[...] = jnp.where(live_row, request_row, first_request)
        live_ref[...] = count(live_row, 1)
        placed_row = jnp.where(
            live_row, holder_row * capacity + holder_rank, -1
        )
        asked = jnp.sum(
            jnp.where(placed_row == iota((slots, entries), 0), local_row + 1, 0).astype(jnp.float32),
            axis=1,
            keepdims=True,
        )
        lane = iota((slots, LANES), 1)
        notes = jnp.where(lane == 0, windows - 1.0, jnp.where(lane == 1, asked - 1.0, 0.0))
        payload_ref[:, vit:] = notes.astype(jnp.bfloat16)

        widened = embedded_ref[...].astype(jnp.float32)
        factor = lax.rsqrt(jnp.mean(widened * widened, axis=1, keepdims=True) + 1e-06)
        normed = (widened * factor * gain_ref[...]).astype(jnp.bfloat16)
        payload_ref[:, :vit] = jnp.dot(
            placed.astype(jnp.bfloat16), normed, preferred_element_type=jnp.float32
        ).astype(jnp.bfloat16)


def embed_and_route(patches, w_patch, vit_gain, row_owner, window_slot, block_table, capacity, slots, per_owner, blocks_dev):
    rows, patch = patches.shape
    vit = w_patch.shape[1]
    entries = block_table.shape[1]
    width = 2 * LANES
    whole = lambda *shape: pl.BlockSpec(shape, lambda step: (0,) * len(shape))
    return pl.pallas_call(
        functools.partial(embed_kernel, capacity, per_owner, blocks_dev),
        grid=(vit // width,),
        out_shape=(
            jax.ShapeDtypeStruct((slots, vit + LANES), jnp.bfloat16),
            jax.ShapeDtypeStruct((rows, 1), jnp.int32),
            jax.ShapeDtypeStruct((1, entries), jnp.int32),
            jax.ShapeDtypeStruct((1, 1), jnp.int32),
        ),
        in_specs=[
            whole(rows, patch),
            pl.BlockSpec((patch, width), lambda step: (0, step)),
            whole(1, vit),
            whole(rows, 1),
            whole(1, rows),
            whole(1, entries),
        ],
        out_specs=(whole(slots, vit + LANES), whole(rows, 1), whole(1, entries), whole(1, 1)),
        scratch_shapes=[pltpu.VMEM((rows, vit), jnp.bfloat16)],
        compiler_params=pltpu.CompilerParams(vmem_limit_bytes=VMEM_BYTES),
        cost_estimate=pl.CostEstimate(
            flops=2 * rows * patch * vit + 2 * slots * rows * vit,
            bytes_accessed=2 * patch * vit + 2 * rows * patch + 2 * slots * vit,
            transcendentals=rows,
        ),
        name="embed_and_route",
    )(patches, w_patch, vit_gain.reshape(1, vit), row_owner, window_slot.reshape(1, rows), block_table)


def prompt_kernel(
    request_ref, live_ref, query_ref, fresh_ref, blocks_ref, out_ref, kv_ref, top_ref, sum_ref, sems
):
    tokens = query_ref.shape[0]
    block_tokens = kv_ref.shape[1]
    kv_width = KVH * HD
    group_size = QHEADS // KVH
    chunk_keys = CHUNK_BLOCKS * block_tokens
    tile_rows = HEADS_TILE * tokens
    live_blocks = live_ref[0, 0]
    chunks = (live_blocks + (CHUNK_BLOCKS - 1)) // CHUNK_BLOCKS

    def fetch(chunk, carry):
        def one(place, inner):
            entry = chunk * CHUNK_BLOCKS + place
            pltpu.make_async_copy(
                blocks_ref.at[request_ref[0, entry]], kv_ref.at[entry], sems.at[chunk]
            ).start()
            return inner

        return lax.fori_loop(0, CHUNK_BLOCKS, one, carry)

    lax.fori_loop(0, chunks, fetch, 0)

    def tiles():
        for group in range(KVH):
            for part in range(group_size // HEADS_TILE):
                yield group, part, group * group_size + part * HEADS_TILE

    def tile_queries(head):
        return jnp.concatenate(
            [query_ref[:, (head + i) * HD : (head + i + 1) * HD] for i in range(HEADS_TILE)], axis=0
        )

    def scores_of(head, keys):
        return lax.dot_general(
            tile_queries(head), keys, (((1,), (1,)), ((), ())), preferred_element_type=jnp.float32
        ) * (HD ** (-0.5) * LOG2E)

    def with_ones(values):
        return jnp.concatenate([values, jnp.ones_like(values)], axis=1)

    causal = iota((tokens, tokens), 1) <= iota((tokens, tokens), 0)
    causal = jnp.concatenate([causal.astype(jnp.int32)] * HEADS_TILE, axis=0) > 0
    for group, part, head in tiles():
        row = head * tokens
        keys = fresh_ref[:, group * HD : (group + 1) * HD]
        values = fresh_ref[:, kv_width + group * HD : kv_width + (group + 1) * HD]
        scores = jnp.where(causal, scores_of(head, keys), HIDDEN)
        top = jnp.max(scores, axis=1, keepdims=True)
        weights = jnp.exp2(scores - top).astype(jnp.bfloat16)
        top_ref[row : row + tile_rows, :] = jnp.broadcast_to(top, (tile_rows, HD))
        sum_ref[row : row + tile_rows, :] = jnp.dot(
            weights, with_ones(values), preferred_element_type=jnp.float32
        )

    def visit(chunk, carry):
        first = chunk * CHUNK_BLOCKS
        pltpu.make_async_copy(
            blocks_ref.at[pl.ds(0, CHUNK_BLOCKS)], kv_ref.at[pl.ds(first, CHUNK_BLOCKS)], sems.at[chunk]
        ).wait()
        shown = iota((1, chunk_keys), 1) < (live_blocks - first) * block_tokens
        for group, part, head in tiles():
            row = head * tokens
            keys = kv_ref[pl.ds(first, CHUNK_BLOCKS), :, group * HD : (group + 1) * HD]
            values = kv_ref[
                pl.ds(first, CHUNK_BLOCKS), :, kv_width + group * HD : kv_width + (group + 1) * HD
            ]
            keys = keys.reshape(chunk_keys, HD)
            values = values.reshape(chunk_keys, HD)
            scores = jnp.where(shown, scores_of(head, keys), HIDDEN)
            old_top = top_ref[row : row + tile_rows, :]
            top = jnp.maximum(old_top, jnp.max(scores, axis=1, keepdims=True))
            shrink = jnp.exp2(old_top - top)
            weights = jnp.exp2(scores - jnp.concatenate([top] * (chunk_keys // HD), axis=1))
            top_ref[row : row + tile_rows, :] = top
            sum_ref[row : row + tile_rows, :] = sum_ref[row : row + tile_rows, :] * jnp.concatenate(
                [shrink, shrink], axis=1
            ) + jnp.dot(
                weights.astype(jnp.bfloat16), with_ones(values), preferred_element_type=jnp.float32
            )
        return carry

    lax.fori_loop(0, chunks, visit, 0)

    for head in range(QHEADS):
        blended = sum_ref[head * tokens : (head + 1) * tokens, :]
        out_ref[:, head * HD : (head + 1) * HD] = (blended[:, :HD] / blended[:, HD:]).astype(jnp.bfloat16)


def prompt_attention(request, live, queries, new_kv, blocks):
    tokens, width = queries.shape
    entries = request.shape[1]
    block_tokens = blocks.shape[1]
    chunks = -(-entries // CHUNK_BLOCKS)
    keys = entries * block_tokens + tokens
    whole = lambda *shape: pl.BlockSpec(shape, lambda *_: (0,) * len(shape))
    return pl.pallas_call(
        prompt_kernel,
        out_shape=jax.ShapeDtypeStruct((tokens, width), jnp.bfloat16),
        grid_spec=pltpu.PrefetchScalarGridSpec(
            num_scalar_prefetch=2,
            grid=(1,),
            in_specs=[
                whole(tokens, width),
                whole(tokens, new_kv.shape[1]),
                pl.BlockSpec(memory_space=pl.ANY),
            ],
            out_specs=whole(tokens, width),
            scratch_shapes=[
                pltpu.VMEM((chunks * CHUNK_BLOCKS, block_tokens, new_kv.shape[1]), jnp.bfloat16),
                pltpu.VMEM((QHEADS * tokens, HD), jnp.float32),
                pltpu.VMEM((QHEADS * tokens, 2 * HD), jnp.float32),
                pltpu.SemaphoreType.DMA((chunks,)),
            ],
        ),
        compiler_params=pltpu.CompilerParams(vmem_limit_bytes=VMEM_BYTES),
        cost_estimate=pl.CostEstimate(
            flops=4 * tokens * keys * width,
            bytes_accessed=4 * tokens * width + 2 * keys * new_kv.shape[1],
            transcendentals=tokens * QHEADS * keys,
        ),
        name="prompt_attention",
    )(request, live, queries, new_kv, blocks)


def pick_kernel(target_ref, returned_ref, out_ref):
    rows, slots = target_ref.shape[0], returned_ref.shape[0]
    picked = (target_ref[...] == iota((rows, slots), 1)).astype(jnp.bfloat16)
    out_ref[...] = jnp.dot(
        picked, returned_ref[...], preferred_element_type=jnp.float32
    ).astype(jnp.bfloat16)


def pick_rows(target, returned):
    return pl.pallas_call(
        pick_kernel,
        out_shape=jax.ShapeDtypeStruct((target.shape[0], returned.shape[1]), jnp.bfloat16),
        compiler_params=pltpu.CompilerParams(vmem_limit_bytes=VMEM_BYTES),
        name="pick_rows",
    )(target, returned)


def window_attention(qkv_rows, windows):
    total_rows = qkv_rows.shape[0]
    inner_width = VHEADS * VHD
    query_heads = qkv_rows[:, :inner_width].reshape(total_rows, VHEADS, VHD)
    key_heads = qkv_rows[:, inner_width : 2 * inner_width].reshape(total_rows, VHEADS, VHD)
    value_heads = qkv_rows[:, 2 * inner_width :].reshape(total_rows, VHEADS, VHD)
    is_live = windows >= 0
    every_row = jnp.arange(total_rows)
    scores = jnp.einsum(
        "qhd,khd->hqk", query_heads, key_heads, preferred_element_type=jnp.float32
    ) * VHD ** (-0.5)
    allowed = (windows[:, None] == windows[None, :]) & is_live[None, :] | (
        every_row[:, None] == every_row[None, :]
    )
    scores = jnp.where(allowed[None], scores, -jnp.inf)
    highest = jnp.max(scores, axis=2, keepdims=True)
    weights = jnp.exp(scores - highest)
    totals = jnp.sum(weights, axis=2)
    blended = jnp.einsum(
        "hqk,khd->qhd",
        weights.astype(jnp.bfloat16),
        value_heads,
        preferred_element_type=jnp.float32,
    )
    pieces = (blended / totals.T[:, :, None]).reshape(total_rows, inner_width)
    return pieces.astype(jnp.bfloat16)


def exchange(rows, devices):
    parts = rows.reshape((devices, rows.shape[0] // devices) + rows.shape[1:])
    return lax.all_to_all(parts, "seq", split_axis=0, concat_axis=0, tiled=True).reshape(rows.shape)


def shards(
    patches,
    row_owner,
    window_slot,
    w_patch,
    vit_gain,
    w_qkv,
    queries,
    new_kv,
    kv_cache,
    block_table,
):
    devices = lax.axis_size("seq")
    vit = w_patch.shape[1]
    capacity = 2 * patches.shape[0] // devices
    slots = devices * capacity
    per_owner = 2 * block_table.shape[1] // devices
    payload, target, request, live = embed_and_route(
        patches, w_patch, vit_gain, row_owner, window_slot, block_table,
        capacity, slots, per_owner, kv_cache.shape[0],
    )
    arrived = exchange(payload, devices)
    notes = arrived[:, vit : vit + 2].astype(jnp.int32)
    asked = notes[:, 1].reshape(devices, capacity)[:, :per_owner].reshape(devices * per_owner)
    fetched = kv_cache[jnp.maximum(asked, 0)]
    delivered = exchange(fetched, devices)
    qkv_rows = jnp.dot(arrived[:, :vit], w_qkv, preferred_element_type=jnp.float32).astype(jnp.bfloat16)
    attended = window_attention(qkv_rows, notes[:, 0])
    delivered, attended = lax.optimization_barrier((delivered, attended))
    returned = exchange(attended, devices)
    attention_out = prompt_attention(request, live, queries, new_kv, delivered)
    vision_out = pick_rows(target, returned)
    return (vision_out, attention_out)


def solution(mesh):
    in_specs = (
        P(("groups", "seq"), None),
        P(("groups", "seq"), None),
        P(("groups", "seq")),
        P(),
        P(),
        P(),
        P(("groups", "seq"), None),
        P(("groups", "seq"), None),
        P(("groups", "seq"), None, None),
        P(("groups", "seq"), None),
    )
    out_specs = (P(("groups", "seq"), None), P(("groups", "seq"), None))
    return jax.shard_map(shards, mesh=mesh, in_specs=in_specs, out_specs=out_specs, check_vma=False)
```

time: 195 us -> 155 us (0.79)
  blocking collectives: 0 us -> 24.1 us
  matrix products: 27.9 us -> 5.08 us
  waiting for transfers between devices: 107 us -> 86.1 us
  starting transfers between devices: 29.7 us -> 10.6 us
  Pallas kernels: 0 us -> 14.7 us
  other arithmetic: 14.4 us -> 0.61 us
  local copies, waits for them, and re-layouts: 14.1 us -> 11.8 us
    all_to_all x0 -> x1, blocking collectives: none -> 24.1 us  [exchange(): lax.all_to_all(parts, 'seq', split_axis=0, concat_axis=0, tiled=True)]
    dot_general x11 -> x1, matrix products: 26.7 us -> 3.93 us  [shards(): jnp.dot(arrived[:, :vit], w_qkv, preferred_element_type=jnp.float32)]
    all_to_all x5 -> x2, waiting for transfers between devices: 107 us -> 86.1 us  [exchange(): lax.all_to_all(parts, 'seq', split_axis=0, concat_axis=0, tiled=True)]
    all_to_all x5 -> x2, starting transfers between devices: 29.7 us -> 10.6 us  [exchange(): lax.all_to_all(parts, 'seq', split_axis=0, concat_axis=0, tiled=True)]
    pallas_call x0 -> x3, Pallas kernels: none -> 14.7 us  [the longest x1 11.2 us: prompt_attention(): pl.pallas_call(prompt_kernel, out_shape=jax.ShapeDtypeStruct((tokens, wid...]
    unnamed x16 -> x15, local copies, waits for them, and re-layouts: 0.78 us -> 6.37 us
    reduce_sum x6 -> x0, other arithmetic: 4.99 us -> none  [the longest x4 4.66 us: prompt_attention(): totals = jnp.sum(weights, axis=2)]
    concatenate x2 -> x0, other arithmetic: 4.4 us -> none  [the longest x1 2.25 us: prompt_attention(): jnp.concatenate([jnp.broadcast_to(cached_live[None, :], (token_count, cac...]
  transfers between devices with their start and end apart: 5 -> 2, of which waited for: 3 -> 1; matrix products, arithmetic and copies ran while one was open for 12% -> 4% of each run, Pallas kernels for 0% -> 7%
where the time goes in v1:
time: 155 us; the launch traced here: 154 us
  waiting for transfers between devices  86.1 us (56%)
  blocking collectives  24.1 us (16%)
  Pallas kernels  14.7 us (9%)
  local copies, waits for them, and re-layouts  11.8 us (8%)
  starting transfers between devices  10.6 us (7%)
  matrix products  5.08 us (3%)
    all_to_all x2, waiting for transfers between devices, exchange(): lax.all_to_all(parts, 'seq', split_axis=0, concat_axis=0, tiled=True)  86.1 us
    all_to_all x1, blocking collectives, exchange(): lax.all_to_all(parts, 'seq', split_axis=0, concat_axis=0, tiled=True)  24.1 us
    pallas_call x1, Pallas kernels, prompt_attention(): pl.pallas_call(prompt_kernel, out_shape=jax.ShapeDtypeStruct((tokens, wid...  11.2 us
    all_to_all x2, starting transfers between devices, exchange(): lax.all_to_all(parts, 'seq', split_axis=0, concat_axis=0, tiled=True)  10.6 us
    unnamed x15, local copies, waits for them, and re-layouts  6.37 us
    dot_general x1, matrix products, shards(): jnp.dot(arrived[:, :vit], w_qkv, preferred_element_type=jnp.float32)  3.93 us
  transfers between devices with their start and end apart: 2, of which 1 were waited for; matrix products, arithmetic and copies ran while one was open for 4% of the time, Pallas kernels for 7%

profile of v1, /device:TPU:13, one launch (start us, length us, event | category | flops | bytes accessed | tf_op | source)
XLA Modules:
  0.0 153.8 jit_solution(12816984368265459282)
XLA Ops:
  0.6 0.8 reshape.119.gain_ref
  1.5 0.8 copy.21.owner_ref
  2.3 1.1 copy.20.patches_ref
  3.4 1.8 %copy-done.1 = bf16[1176,1280]{1,0:T(8,128)(2,1)S(1)} copy-done((bf16[1176,1280]{1,0:T(8,128)(2,1)S(1)}, bf16[1176,1280]{1,0:T(8,128)(2,1)}, u32[]{:S(2)}) %copy-start.1) | copy-done | bytes 3010584
  5.3 0.7 copy-done.2
  5.9 0.7 copy-done.3
  6.6 2.5 %embed_and_route.1 = (bf16[256,1408]{1,0:T(8,128)(2,1)S(1)}, s32[128,1]{1,0:T(8,128)S(1)}, s32[1,64]{1,0:T(1,128)S(1)}, s32[1,1]{1,0:T(1,128)}) custom-call(bf16[128,1176]{1,0:T(8,128)(2,1)S(1)} %copy.20.patches_ref, bf16[1176,1280]{1,0:T(8,128)(2,1)S(1)} %copy-done.1, f32[1,1280]{1,0:T(1,128)S(1)} %reshape.119.gain_ref, s32[128,1]{1,0:T(8,128)S(1)} %copy.21.owner_ref, ...), custom_call_target="tpu_custom_call" | custom-call | flops 469237760 | bytes 3966976 | tf_op jit(solution)/shard_map/embed_and_route/pallas_call | solution.py:123
  9.1 24.1 %all_to_all.15 = bf16[16,16,1408]{2,1,0:T(8,128)(2,1)S(1)} all-to-all(bf16[16,16,1408]{2,1,0:T(8,128)(2,1)S(1)} %bitcast.24), channel_id=1, replica_groups=mesh['groups'=2,'seq'=16] {'seq'}, dimensions={0} | all-to-all | bytes 1441792 | tf_op jit(solution)/shard_map/all_to_all | solution.py:325
  33.6 2.8 %gather_fusion = bf16[128,16,1024]{2,1,0:T(8,128)(2,1)} fusion(bf16[64,16,1024]{2,1,0:T(8,128)(2,1)S(1)} %copy-done, s32[1024]{0:T(1024)S(1)} %pad_clamp_fusion), kind=kCustom, calls=%fused_computation | custom fusion | bytes 8389120 | tf_op jit(solution)/shard_map/gather | solution.py:352
  36.4 5.7 %all-to-all-start.1 = ((bf16[16,8,16,1024]{3,2,1,0:T(8,128)(2,1)}), bf16[16,8,16,1024]{3,2,1,0:T(8,128)(2,1)}, u32[]{:S(2)}, u32[]{:S(2)}) async-start(bf16[16,8,16,1024]{3,2,1,0:T(8,128)(2,1)} %bitcast.26), calls=%async_computation.1 | async-start | bytes 8388608 | tf_op jit(solution)/shard_map/all_to_all | solution.py:325
  42.1 3.9 %convolution_convert_fusion = bf16[256,1920]{1,0:T(8,128)(2,1)S(1)} fusion(bf16[1280,1920]{1,0:T(8,128)(2,1)} %param.15, bf16[256,1408]{1,0:T(8,128)(2,1)S(1)} %bitcast.30), kind=kOutput, calls=%fused_computation.1 | convolution fusion | flops 1258782720 | bytes 6553600 | tf_op jit(solution)/shard_map/dot_general | solution.py:354
  46.1 0.2 copy.25
  46.3 0.2 copy.24
  46.5 0.2 copy.23
  46.7 0.1 fusion.11
  46.9 0.5 fusion
  47.4 0.4 fusion.1
  47.9 0.6 fusion.4
  48.5 86.1 %all-to-all-done.1 = bf16[16,8,16,1024]{3,2,1,0:T(8,128)(2,1)} async-done(((bf16[16,8,16,1024]{3,2,1,0:T(8,128)(2,1)}), bf16[16,8,16,1024]{3,2,1,0:T(8,128)(2,1)}, u32[]{:S(2)}, u32[]{:S(2)}) %all-to-all-start.1) | async-done | bytes 4194336 | tf_op jit(solution)/shard_map/all_to_all | solution.py:325
  134.6 0.9 copy.27
  135.5 4.9 %all-to-all-start.2 = ((bf16[16,16,640]{2,1,0:T(8,128)(2,1)}), bf16[16,16,640]{2,1,0:T(8,128)(2,1)S(1)}, u32[]{:S(2)}, u32[]{:S(2)}) async-start(bf16[16,16,640]{2,1,0:T(8,128)(2,1)} %bitcast.12), calls=%async_computation.2 | async-start | bytes 655360 | tf_op jit(solution)/shard_map/all_to_all | solution.py:325
  140.4 1.2 copy-done.4
  141.6 11.2 %prompt_attention.1 = bf16[128,4096]{1,0:T(8,128)(2,1)} custom-call(s32[1,64]{1,0:T(1,128)S(1)} %get-tuple-element.11.request_ref, s32[1,1]{1,0:T(1,128)} %get-tuple-element.12.live_ref, bf16[128,4096]{1,0:T(8,128)(2,1)S(1)} %copy-done.4, bf16[128,1024]{1,0:T(8,128)(2,1)S(1)} %copy-done.5, bf16[128,16,1024]{2,1,0:T(8,128)(2,1)} %bitcast.4.blocks_ref), custom_call_target="tpu_custom_call" | custom-call | flops 2415919104 | bytes 4456448 | tf_op jit(solution)/shard_map/prompt_attention/pallas_call | solution.py:249
  152.8 0.9 pick_rows.1
  (19 shorter events, 0.4 us)
Async XLA Ops:
  0.6 33.0 %copy-start = (bf16[64,16,1024]{2,1,0:T(8,128)(2,1)S(1)}, bf16[64,16,1024]{2,1,0:T(8,128)(2,1)}, u32[]{:S(2)}) copy-start(bf16[64,16,1024]{2,1,0:T(8,128)(2,1)} %param.18) | copy-start | bytes 6291460
  3.4 1.9 %copy-start.1 = (bf16[1176,1280]{1,0:T(8,128)(2,1)S(1)}, bf16[1176,1280]{1,0:T(8,128)(2,1)}, u32[]{:S(2)}) copy-start(bf16[1176,1280]{1,0:T(8,128)(2,1)} %w_ref.1) | copy-start | bytes 9031684
  5.2 0.7 copy-start.2
  5.9 0.7 copy-start.3
  36.4 98.2 %all-to-all-start.1 = ((bf16[16,8,16,1024]{3,2,1,0:T(8,128)(2,1)}), bf16[16,8,16,1024]{3,2,1,0:T(8,128)(2,1)}, u32[]{:S(2)}, u32[]{:S(2)}) async-start(bf16[16,8,16,1024]{3,2,1,0:T(8,128)(2,1)} %bitcast.26), calls=%async_computation.1 | async-start | bytes 8388608 | tf_op jit(solution)/shard_map/all_to_all | solution.py:325
  47.9 92.5 %copy-start.5 = (bf16[128,1024]{1,0:T(8,128)(2,1)S(1)}, bf16[128,1024]{1,0:T(8,128)(2,1)}, u32[]{:S(2)}) copy-start(bf16[128,1024]{1,0:T(8,128)(2,1)} %fresh_ref.1) | copy-start | bytes 786436
  135.5 17.3 %all-to-all-start.2 = ((bf16[16,16,640]{2,1,0:T(8,128)(2,1)}), bf16[16,16,640]{2,1,0:T(8,128)(2,1)S(1)}, u32[]{:S(2)}, u32[]{:S(2)}) async-start(bf16[16,16,640]{2,1,0:T(8,128)(2,1)} %bitcast.12), calls=%async_computation.2 | async-start | bytes 655360 | tf_op jit(solution)/shard_map/all_to_all | solution.py:325
  140.4 1.2 copy-start.4
